TPU v7x, 32 devices: a whole 2x2x4 slice. The times are simulated.
32 devices in a mesh: pix: 8 (over z, core), date: 4 (over y, x).
Axes of the slice: x: 2, y: 2, z: 4, core: 2. Of those that a mesh axis runs over, the one named last changes fastest.
Arguments:
- pixel_factor: float32 [16384, 256], P(('pix', 'date')), may hold values from -1.5 to 1.5
- date_factor: float32 [3072, 256], P(('date', 'pix')), may hold values from -1.5 to 1.5
- clear_obs: bfloat16 [8, 4, 32, 128, 128], P('pix', 'date'), may hold values from -6 to 6
- clear_blocks: int32 [8, 4, 32], P('pix', 'date'), may hold values from 0 to 95, as said below
- clear_count: int32 [8, 4], P('pix', 'date'), may hold values from 1 to 32, as said below
Outputs:
- pixel_next: float32 [16384, 256], P(('pix', 'date'))
- date_next: float32 [3072, 256], P(('date', 'pix'))
Inputs may be any that keep to these rules, and one draw needn't show every extreme that they name: `clear_blocks`: within one tile the 32 entries are distinct block numbers; only the first clear_count entries are clear blocks, later slots carry no observations. `clear_count`: counts are uneven over tiles; at least one tile has exactly 32 clear blocks.
All inputs are finite; a program needn't handle non-finite values.
Results may differ from a plain program's by a relative error of at most 0.013.
Values may be sent and summed in bfloat16 or wider, within the bound.
A program may use at most 64 MiB of HBM per device.

v0:
```python
import jax
import jax.numpy as jnp
from jax import lax
from jax.sharding import PartitionSpec as P

BLOCK = 128
ITERS = 2


def block_terms(pixel_panel, date_panel, observed, blocks, filled):
    rank_width = pixel_panel.shape[1]
    row_blocks = pixel_panel.shape[0] // BLOCK
    col_blocks = date_panel.shape[0] // BLOCK
    capacity = blocks.shape[0]
    row_index = blocks // col_blocks
    col_index = blocks % col_blocks
    pixel_tiles = pixel_panel.reshape(row_blocks, BLOCK, rank_width)[row_index]
    date_tiles = date_panel.reshape(col_blocks, BLOCK, rank_width)[col_index]
    predicted = jnp.einsum(
        "kir,kjr->kij", pixel_tiles, date_tiles, preferred_element_type=jnp.float32
    )
    living = (jnp.arange(capacity) < filled)[:, None, None]
    misfit = jnp.where(living, predicted - observed.astype(jnp.float32), 0.0).astype(jnp.bfloat16)
    pixel_terms = jnp.einsum("kij,kjr->kir", misfit, date_tiles, preferred_element_type=jnp.float32)
    date_terms = jnp.einsum("kij,kir->kjr", misfit, pixel_tiles, preferred_element_type=jnp.float32)
    pixel_grad = (
        jnp.zeros((row_blocks, BLOCK, rank_width), jnp.float32).at[row_index].add(pixel_terms)
    )
    date_grad = (
        jnp.zeros((col_blocks, BLOCK, rank_width), jnp.float32).at[col_index].add(date_terms)
    )
    return (pixel_grad.reshape(-1, rank_width), date_grad.reshape(-1, rank_width))


def shards(pixel_factor, date_factor, clear_obs, clear_blocks, clear_count):
    observed = clear_obs[0, 0]
    blocks = clear_blocks[0, 0]
    filled = clear_count[0, 0]
    devices = lax.axis_size("pix") * lax.axis_size("date")
    rate_pixel = 64.0 / (date_factor.shape[0] * devices)
    rate_date = 64.0 / (pixel_factor.shape[0] * devices)
    pixel_now = pixel_factor
    date_now = date_factor
    for step in range(ITERS):
        pixel_panel = lax.all_gather(pixel_now.astype(jnp.bfloat16), "date", axis=0, tiled=True)
        date_panel = lax.all_gather(date_now.astype(jnp.bfloat16), "pix", axis=0, tiled=True)
        pixel_grad, date_grad = block_terms(pixel_panel, date_panel, observed, blocks, filled)
        pixel_now = pixel_now - rate_pixel * lax.psum_scatter(
            pixel_grad.astype(jnp.bfloat16), "date", scatter_dimension=0, tiled=True
        ).astype(jnp.float32)
        date_now = date_now - rate_date * lax.psum_scatter(
            date_grad.astype(jnp.bfloat16), "pix", scatter_dimension=0, tiled=True
        ).astype(jnp.float32)
    return (pixel_now, date_now)


def solution(mesh):
    in_specs = (
        P(("pix", "date"), None),
        P(("date", "pix"), None),
        P("pix", "date", None, None, None),
        P("pix", "date", None),
        P("pix", "date"),
    )
    out_specs = (P(("pix", "date"), None), P(("date", "pix"), None))
    return jax.shard_map(shards, mesh=mesh, in_specs=in_specs, out_specs=out_specs, check_vma=False)
```

profile of v0, /device:TPU:0, one launch (start us, length us, event | category | flops | bytes accessed | tf_op | source)
XLA Modules:
  0.0 228.5 jit_solution(5775017426684024150)
XLA Ops:
  7.2 1.8 convert_element_type.61
  11.3 16.2 %all_gather.13 = bf16[768,256]{1,0:T(8,128)(2,1)S(1)} all-gather(bf16[96,256]{1,0:T(8,128)(2,1)S(1)} %convert_element_type.62), channel_id=1, replica_groups=mesh['pix'=8,'date'=4] {'pix'}, dimensions={0}, use_global_device_ids=true | all-gather | bytes 442368 | tf_op jit(solution)/shard_map/all_gather | solution.py:46
  27.5 2.0 gather_fusion.1
  29.5 10.2 %all-gather.3.cloned.1.call-done = bf16[2048,256]{1,0:T(8,128)(2,1)} async-done(((bf16[512,256]{1,0:T(8,128)(2,1)}), bf16[2048,256]{1,0:T(8,128)(2,1)}) %all-gather.3.cloned.1.call-update) | async-done | bytes 1048592 | tf_op jit(solution)/shard_map/all_gather | solution.py:45
  39.8 1.9 gather_fusion
  41.7 3.1 %fusion.33 = f32[32,128,128]{2,1,0:T(8,128)S(1)} fusion(bf16[32,128,256]{2,1,0:T(8,128)(2,1)S(1)} %gather_fusion, bf16[32,128,256]{2,1,0:T(8,128)(2,1)} %gather_fusion.1), kind=kOutput, calls=%fused_computation.50 | convolution fusion | flops 268435456 | bytes 6291456 | tf_op jit(solution)/shard_map/kir,kjr->kij/dot_general | solution.py:19
  44.9 2.7 %fusion.10 = f32[32,128,256]{2,1,0:T(8,128)} fusion(bf16[32,128,256]{2,1,0:T(8,128)(2,1)S(1)} %copy-done.2, f32[32,128,128]{2,1,0:T(8,128)S(1)} %fusion.33, bf16[1,1,32,128,128]{4,3,2,1,0:T(8,128)(2,1)S(1)} %copy-done.4, pred[32]{0:T(512)(128)(4,1)S(1)} %iota_compare_fusion), kind=kOutput, calls=%fused_computation.17 | convolution fusion | flops 270532608 | bytes 9437216 | tf_op jit(solution)/shard_map/kij,kjr->kir/dot_general | solution.py:24
  47.9 6.5 %scatter_fusion = f32[16,128,256]{2,1,0:T(8,128)S(1)} fusion(f32[16,128,256]{2,1,0:T(8,128)S(1)} %broadcast.115.clone, s32[32]{0:T(128)S(1)} %get-tuple-element.3, f32[32,128,256]{2,1,0:T(8,128)} %fusion.10), kind=kCustom, calls=%fused_computation.4 | custom fusion | flops 1048576 | bytes 12583040 | tf_op jit(solution)/shard_map/scatter-add | solution.py:27
  55.6 5.1 %fusion.8 = f32[32,128,256]{2,1,0:T(8,128)} fusion(bf16[32,128,256]{2,1,0:T(8,128)(2,1)} %copy-done.1, f32[32,128,128]{2,1,0:T(8,128)} %copy-done, bf16[1,1,32,128,128]{4,3,2,1,0:T(8,128)(2,1)S(1)} %copy-done.4, pred[32]{0:T(512)(128)(4,1)S(1)} %iota_compare_fusion), kind=kOutput, calls=%fused_computation.16 | convolution fusion | flops 270532608 | bytes 9437216 | tf_op jit(solution)/shard_map/kij,kir->kjr/dot_general | solution.py:25
  60.8 6.6 %scatter_fusion.1 = f32[6,128,256]{2,1,0:T(8,128)S(1)} fusion(f32[6,128,256]{2,1,0:T(8,128)S(1)} %broadcast.118.clone, s32[32]{0:T(128)S(1)} %get-tuple-element.2, f32[32,128,256]{2,1,0:T(8,128)} %fusion.8), kind=kCustom, calls=%fused_computation.5 | custom fusion | flops 1048576 | bytes 12583040 | tf_op jit(solution)/shard_map/scatter-add | solution.py:30
  68.3 15.2 %reduce-scatter.5.cloned.1.call-done = bf16[512,256]{1,0:T(8,128)(2,1)} async-done(((bf16[2048,256]{1,0:T(8,128)(2,1)}), bf16[512,256]{1,0:T(8,128)(2,1)}) %reduce-scatter.5.cloned.1.call-update) | async-done | bytes 262160 | tf_op jit(solution)/shard_map/reduce_scatter | solution.py:48
  85.2 31.8 %reduce-scatter.7.cloned.1.call-done = bf16[96,256]{1,0:T(8,128)(2,1)} async-done(((bf16[768,256]{1,0:T(8,128)(2,1)}), bf16[96,256]{1,0:T(8,128)(2,1)}) %reduce-scatter.7.cloned.1.call-update) | async-done | bytes 49168 | tf_op jit(solution)/shard_map/reduce_scatter | solution.py:51
  117.9 14.5 %all_gather.15 = bf16[768,256]{1,0:T(8,128)(2,1)S(1)} all-gather(bf16[96,256]{1,0:T(8,128)(2,1)S(1)} %fusion.25), channel_id=1, replica_groups=mesh['pix'=8,'date'=4] {'pix'}, dimensions={0}, use_global_device_ids=true | all-gather | bytes 442368 | tf_op jit(solution)/shard_map/all_gather | solution.py:46
  132.4 2.0 gather_fusion.3
  134.3 9.2 %all-gather.5.cloned.1.call-done = bf16[2048,256]{1,0:T(8,128)(2,1)} async-done(((bf16[512,256]{1,0:T(8,128)(2,1)}), bf16[2048,256]{1,0:T(8,128)(2,1)}) %all-gather.5.cloned.1.call-update) | async-done | bytes 1048592 | tf_op jit(solution)/shard_map/all_gather | solution.py:45
  143.6 3.3 %gather_fusion.2 = bf16[32,128,256]{2,1,0:T(8,128)(2,1)} fusion(bf16[16,128,256]{2,1,0:T(8,128)(2,1)} %bitcast.60, s32[1024]{0:T(1024)S(1)} %get-tuple-element.5), kind=kCustom, calls=%fused_computation.2 | custom fusion | bytes 4194432 | tf_op jit(solution)/shard_map/gather | solution.py:17
  146.8 3.1 %fusion.34 = f32[32,128,128]{2,1,0:T(8,128)S(1)} fusion(bf16[32,128,256]{2,1,0:T(8,128)(2,1)} %gather_fusion.2, bf16[32,128,256]{2,1,0:T(8,128)(2,1)} %gather_fusion.3), kind=kOutput, calls=%fused_computation.51 | convolution fusion | flops 268435456 | bytes 6291456 | tf_op jit(solution)/shard_map/kir,kjr->kij/dot_general | solution.py:19
  149.9 2.9 %fusion.4 = f32[32,128,256]{2,1,0:T(8,128)} fusion(bf16[32,128,256]{2,1,0:T(8,128)(2,1)S(1)} %copy-done.3, f32[32,128,128]{2,1,0:T(8,128)S(1)} %fusion.34, bf16[1,1,32,128,128]{4,3,2,1,0:T(8,128)(2,1)S(1)} %copy-done.4, pred[32]{0:T(512)(128)(4,1)S(1)} %iota_compare_fusion), kind=kOutput, calls=%fused_computation.14 | convolution fusion | flops 270532608 | bytes 9437216 | tf_op jit(solution)/shard_map/kij,kir->kjr/dot_general | solution.py:25
  152.9 6.4 %scatter_fusion.3 = f32[6,128,256]{2,1,0:T(8,128)S(1)} fusion(f32[6,128,256]{2,1,0:T(8,128)S(1)} %broadcast.118, s32[32]{0:T(128)S(1)} %get-tuple-element.2, f32[32,128,256]{2,1,0:T(8,128)} %fusion.4), kind=kCustom, calls=%fused_computation.7 | custom fusion | flops 1048576 | bytes 12583040 | tf_op jit(solution)/shard_map/scatter-add | solution.py:30
  160.4 4.6 %fusion.6 = f32[32,128,256]{2,1,0:T(8,128)} fusion(bf16[32,128,256]{2,1,0:T(8,128)(2,1)} %gather_fusion.3, f32[32,128,128]{2,1,0:T(8,128)S(1)} %fusion.34, bf16[1,1,32,128,128]{4,3,2,1,0:T(8,128)(2,1)} %param.7, pred[32]{0:T(512)(128)(4,1)S(1)} %iota_compare_fusion), kind=kOutput, calls=%fused_computation.15 | convolution fusion | flops 270532608 | bytes 9437216 | tf_op jit(solution)/shard_map/kij,kjr->kir/dot_general | solution.py:24
  165.2 6.5 %scatter_fusion.2 = f32[16,128,256]{2,1,0:T(8,128)S(1)} fusion(f32[16,128,256]{2,1,0:T(8,128)S(1)} %broadcast.115, s32[32]{0:T(128)S(1)} %get-tuple-element.3, f32[32,128,256]{2,1,0:T(8,128)} %fusion.6), kind=kCustom, calls=%fused_computation.6 | custom fusion | flops 1048576 | bytes 12583040 | tf_op jit(solution)/shard_map/scatter-add | solution.py:27
  172.9 18.0 %reduce-scatter.11.cloned.1.call-done = bf16[96,256]{1,0:T(8,128)(2,1)} async-done(((bf16[768,256]{1,0:T(8,128)(2,1)}), bf16[96,256]{1,0:T(8,128)(2,1)}) %reduce-scatter.11.cloned.1.call-update) | async-done | bytes 49168 | tf_op jit(solution)/shard_map/reduce_scatter | solution.py:51
  192.4 27.5 %reduce-scatter.9.cloned.1.call-done = bf16[512,256]{1,0:T(8,128)(2,1)} async-done(((bf16[2048,256]{1,0:T(8,128)(2,1)}), bf16[512,256]{1,0:T(8,128)(2,1)}) %reduce-scatter.9.cloned.1.call-update) | async-done | bytes 262160 | tf_op jit(solution)/shard_map/reduce_scatter | solution.py:48
  219.8 1.8 multiply_subtract_fusion
  (47 shorter events, 10.6 us)
Async XLA Ops:
  7.2 32.6 %all-gather.3.cloned.1.call-start = ((), (), s32[]{:S(2)}) async-start(), calls=%async_computation.4 | async-start | bytes 1310720 | tf_op jit(solution)/shard_map/all_gather | solution.py:45
  9.0 74.4 %reduce-scatter.5.cloned.1.call-start = ((), (), s32[]{:S(2)}) async-start(), calls=%async_computation.5 | async-start | bytes 1310720 | tf_op jit(solution)/shard_map/reduce_scatter | solution.py:48
  41.7 3.1 %copy-start.1 = (bf16[32,128,256]{2,1,0:T(8,128)(2,1)}, bf16[32,128,256]{2,1,0:T(8,128)(2,1)S(1)}, u32[]{:S(2)}) copy-start(bf16[32,128,256]{2,1,0:T(8,128)(2,1)S(1)} %gather_fusion) | copy-start | bytes 6291460
  41.7 3.1 %copy-start.2 = (bf16[32,128,256]{2,1,0:T(8,128)(2,1)S(1)}, bf16[32,128,256]{2,1,0:T(8,128)(2,1)}, u32[]{:S(2)}) copy-start(bf16[32,128,256]{2,1,0:T(8,128)(2,1)} %gather_fusion.1) | copy-start | bytes 6291460
  41.7 3.2 %copy-start.4 = (bf16[1,1,32,128,128]{4,3,2,1,0:T(8,128)(2,1)S(1)}, bf16[1,1,32,128,128]{4,3,2,1,0:T(8,128)(2,1)}, u32[]{:S(2)}) copy-start(bf16[1,1,32,128,128]{4,3,2,1,0:T(8,128)(2,1)} %param.7) | copy-start | bytes 3145732
  44.9 2.7 %copy-start = (f32[32,128,128]{2,1,0:T(8,128)}, f32[32,128,128]{2,1,0:T(8,128)S(1)}, u32[]{:S(2)}) copy-start(f32[32,128,128]{2,1,0:T(8,128)S(1)} %fusion.33) | copy-start | bytes 6291460
  55.6 61.5 %reduce-scatter.7.cloned.1.call-start = ((), (), s32[]{:S(2)}) async-start(), calls=%async_computation.7 | async-start | bytes 442368 | tf_op jit(solution)/shard_map/reduce_scatter | solution.py:51
  60.8 22.7 %copy-start.5 = (f32[512,256]{1,0:T(8,128)S(1)}, f32[512,256]{1,0:T(8,128)}, u32[]{:S(2)}) copy-start(f32[512,256]{1,0:T(8,128)} %param.5) | copy-start | bytes 1572868
  67.4 49.7 %copy-start.8 = (f32[96,256]{1,0:T(8,128)S(1)}, f32[96,256]{1,0:T(8,128)}, u32[]{:S(2)}) copy-start(f32[96,256]{1,0:T(8,128)} %param.6) | copy-start | bytes 294916
  68.2 75.3 %all-gather.5.cloned.1.call-start = ((), (), s32[]{:S(2)}) async-start(), calls=%async_computation.6 | async-start | bytes 1310720 | tf_op jit(solution)/shard_map/all_gather | solution.py:45
  85.2 105.7 %reduce-scatter.11.cloned.1.call-start = ((), (), s32[]{:S(2)}) async-start(), calls=%async_computation.9 | async-start | bytes 442368 | tf_op jit(solution)/shard_map/reduce_scatter | solution.py:51
  146.8 3.1 %copy-start.3 = (bf16[32,128,256]{2,1,0:T(8,128)(2,1)S(1)}, bf16[32,128,256]{2,1,0:T(8,128)(2,1)}, u32[]{:S(2)}) copy-start(bf16[32,128,256]{2,1,0:T(8,128)(2,1)} %gather_fusion.2) | copy-start | bytes 6291460
  160.1 59.7 %reduce-scatter.9.cloned.1.call-start = ((), (), s32[]{:S(2)}) async-start(), calls=%async_computation.8 | async-start | bytes 1310720 | tf_op jit(solution)/shard_map/reduce_scatter | solution.py:48
  171.7 19.2 %copy-start.9 = (bf16[96,256]{1,0:T(8,128)(2,1)S(1)}, bf16[96,256]{1,0:T(8,128)(2,1)}, u32[]{:S(2)}) copy-start(bf16[96,256]{1,0:T(8,128)(2,1)} %reduce-scatter.7.cloned.1.call-done) | copy-start | bytes 147460
  171.7 48.1 %copy-start.6 = (f32[512,256]{1,0:T(8,128)S(1)}, f32[512,256]{1,0:T(8,128)}, u32[]{:S(2)}) copy-start(f32[512,256]{1,0:T(8,128)} %param.5) | copy-start | bytes 1572868
  171.7 48.1 %copy-start.7 = (bf16[512,256]{1,0:T(8,128)(2,1)S(1)}, bf16[512,256]{1,0:T(8,128)(2,1)}, u32[]{:S(2)}) copy-start(bf16[512,256]{1,0:T(8,128)(2,1)} %reduce-scatter.5.cloned.1.call-done) | copy-start | bytes 786436
Sparse Core Ops, SparseCore 0:
  10.4 29.3 all-gather.2
  55.7 27.7 reduce-scatter.4
  86.4 30.6 reduce-scatter.6
  118.8 24.7 all-gather.4
  160.3 30.5 reduce-scatter.10
  193.9 25.8 reduce-scatter.8
where the time goes:
time: 229 us
  waiting for transfers between devices  112 us (49%)
  other arithmetic  39.1 us (17%)
  blocking collectives  30.7 us (13%)
  matrix products  21.5 us (9%)
  between operations  14.9 us (7%)
  local copies, waits for them, and re-layouts  9.85 us (4%)
    reduce_scatter x2, waiting for transfers between devices, shards(): lax.psum_scatter(date_grad.astype(jnp.bfloat16), 'pix', scatter_dimension...  49.9 us
    reduce_scatter x2, waiting for transfers between devices, shards(): lax.psum_scatter(pixel_grad.astype(jnp.bfloat16), 'date', scatter_dimensi...  42.6 us
    all_gather x2, blocking collectives, shards(): lax.all_gather(date_now.astype(jnp.bfloat16), 'pix', axis=0, tiled=True)  30.7 us
    all_gather x2, waiting for transfers between devices, shards(): lax.all_gather(pixel_now.astype(jnp.bfloat16), 'date', axis=0, tiled=True)  19.5 us
    scatter-add x2, other arithmetic, block_terms(): jnp.zeros((col_blocks, BLOCK, rank_width), jnp.float32).at[col_index]  13 us
    scatter-add x2, other arithmetic, block_terms(): jnp.zeros((row_blocks, BLOCK, rank_width), jnp.float32).at[row_index]  13 us
    dot_general x2, matrix products, block_terms(): jnp.einsum('kij,kir->kjr', misfit, pixel_tiles, preferred_element_type=jn...  8 us
    dot_general x2, matrix products, block_terms(): jnp.einsum('kij,kjr->kir', misfit, date_tiles, preferred_element_type=jnp...  7.34 us
  transfers between devices with their start and end apart: 6, of which 6 were waited for; matrix products, arithmetic and copies ran while one was open for 15% of the time, Pallas kernels for 0%

commit v1 on v0

v1 whole, which is shorter than its diff:
```python
import functools

import jax
import jax.numpy as jnp
from jax import lax
from jax.experimental import pallas as pl
from jax.experimental.pallas import tpu as pltpu
from jax.sharding import PartitionSpec as P

BLOCK = 128
ITERS = 2
MESH = pl.DeviceIdType.MESH
BF = jnp.bfloat16
F32 = jnp.float32


def dot(a, b, ca, cb):
    return lax.dot_general(a, b, (((ca,), (cb,)), ((), ())), preferred_element_type=F32)


def kernel(
    n_pix, n_date, rate_u, rate_v,
    slot_ref, live_ref, u_ref, v_ref, obs_hbm, u_out, v_out,
    obs, ubuf, vbuf, gus, gur, gvs, gvr, vpan, mbuf, gvt, own_gu,
    obs_sem, us, ur, vs, vr, gu_s, gu_r, gv_s, gv_r,
):
    me_p = lax.axis_index("pix")
    me_d = lax.axis_index("date")
    ru, rank = u_ref.shape
    rv = v_ref.shape[0]
    nb = ru // BLOCK
    cols = n_pix * rv
    cb = cols // BLOCK

    load = pltpu.make_async_copy(obs_hbm, obs, obs_sem)
    load.start()

    def at_date(s):
        return lax.rem(me_d + s, n_date)

    def at_pix(s):
        return lax.rem(me_p + s, n_pix)

    def copy(src, dst, ssem, rsem, p, d):
        return pltpu.make_async_remote_copy(
            src_ref=src, dst_ref=dst, send_sem=ssem, recv_sem=rsem, device_id=(p, d), device_id_type=MESH
        )

    def u_copy(t, s):
        return copy(ubuf.at[t, me_d], ubuf.at[t, me_d], us.at[t, s], ur.at[t, s], me_p, at_date(s))

    def v_copy(t, s):
        return copy(vbuf.at[t, me_p], vbuf.at[t, me_p], vs.at[t, s], vr.at[t, s], at_pix(s), me_d)

    def gu_copy(t, s):
        return copy(gus.at[t, s], gur.at[t, s], gu_s.at[t, s], gu_r.at[t, s], me_p, at_date(s))

    def gv_copy(t, s):
        return copy(gvs.at[t, at_pix(s)], gvr.at[t, s], gv_s.at[t, s], gv_r.at[t, s], at_pix(s), me_d)

    barrier = pltpu.get_barrier_semaphore()
    for s in range(1, n_date):
        pl.semaphore_signal(barrier, inc=1, device_id=(me_p, at_date(s)), device_id_type=MESH)
    for s in range(1, n_pix):
        pl.semaphore_signal(barrier, inc=1, device_id=(at_pix(s), me_d), device_id_type=MESH)
    ubuf[0, me_d] = u_ref[...].astype(BF)
    vbuf[0, me_p] = v_ref[...].astype(BF)
    pl.semaphore_wait(barrier, n_date + n_pix - 2)

    def chunk(t, source, store):
        uc = ubuf.at[t, source]

        def rows(ib, carry):
            first = pl.multiple_of(ib * BLOCK, BLOCK)
            predicted = dot(uc[pl.ds(first, BLOCK), :], vpan[...], 1, 1)
            for j in range(cb):
                b = (source * nb + ib) * cb + j
                o = obs[slot_ref[b]].astype(F32)
                m = (predicted[:, j * BLOCK:(j + 1) * BLOCK] - o) * live_ref[b]
                mbuf[pl.ds(first, BLOCK), j * BLOCK:(j + 1) * BLOCK] = m.astype(BF)
            return carry

        lax.fori_loop(0, nb, rows, 0)
        misfit = mbuf[...]
        store(dot(misfit, vpan[...], 1, 0).astype(BF))
        return dot(uc[...], misfit, 0, 0)

    u_prev, v_prev = u_ref, v_ref
    for t in range(ITERS):
        for s in range(1, n_pix):
            v_copy(t, s).start()
        for s in range(1, n_date):
            u_copy(t, s).start()
        if t == 0:
            load.wait()
        for s in range(1, n_pix):
            v_copy(t, s).wait_recv()
        panel = vbuf[t]
        if rv % 16:
            panel = panel.astype(F32)
        vpan[...] = panel.reshape(cols, rank).astype(BF)

        def keep(g):
            own_gu[...] = g

        gvt[...] = chunk(t, me_d, keep)

        def step(s, carry):
            u_copy(t, n_date - s).wait_recv()

            def send(g):
                gus[t, s] = g

            gvt[...] += chunk(t, at_date(s), send)
            gu_copy(t, s).start()
            return carry

        lax.fori_loop(1, n_date, step, 0)
        gv = gvt[...].T.reshape(n_pix, rv, rank)
        gvs[t] = gv.astype(BF)
        for s in range(1, n_pix):
            gv_copy(t, s).start()

        total = gvs[t, me_p].astype(F32)
        for s in range(1, n_pix):
            gv_copy(t, s).wait_recv()
            total += gvr[t, s].astype(F32)
        v_out[...] = v_prev[...] - rate_v * total
        if t + 1 < ITERS:
            vbuf[t + 1, me_p] = v_out[...].astype(BF)
        total = own_gu[...].astype(F32)
        for s in range(1, n_date):
            gu_copy(t, s).wait_recv()
            total += gur[t, s].astype(F32)
        u_out[...] = u_prev[...] - rate_u * total
        if t + 1 < ITERS:
            ubuf[t + 1, me_d] = u_out[...].astype(BF)
        u_prev, v_prev = u_out, v_out

    for t in range(ITERS):
        for s in range(1, n_pix):
            v_copy(t, s).wait_send()
            gv_copy(t, s).wait_send()
        for s in range(1, n_date):
            u_copy(t, s).wait_send()
            gu_copy(t, s).wait_send()


def shards(n_pix, n_date, pixel_factor, date_factor, clear_obs, clear_blocks, clear_count):
    ru, rank = pixel_factor.shape
    rv = date_factor.shape[0]
    devices = n_pix * n_date
    cap = clear_obs.shape[2]
    cols = n_pix * rv
    blocks_in_tile = (n_date * ru // BLOCK) * (cols // BLOCK)
    match = (clear_blocks[0, 0][None, :] == jnp.arange(blocks_in_tile)[:, None]) & (
        jnp.arange(cap)[None, :] < clear_count[0, 0]
    )
    slot = jnp.sum(jnp.where(match, jnp.arange(cap)[None, :], 0), axis=1).astype(jnp.int32)
    live = jnp.sum(match.astype(F32), axis=1)
    body = functools.partial(
        kernel, n_pix, n_date, 64.0 / (rv * devices), 64.0 / (ru * devices)
    )
    vmem = pl.BlockSpec(memory_space=pltpu.VMEM)
    smem = pl.BlockSpec(memory_space=pltpu.SMEM)
    dma = pltpu.SemaphoreType.DMA
    return pl.pallas_call(
        body,
        out_shape=(
            jax.ShapeDtypeStruct((ru, rank), F32),
            jax.ShapeDtypeStruct((rv, rank), F32),
        ),
        in_specs=[smem, smem, vmem, vmem, pl.BlockSpec(memory_space=pl.ANY)],
        out_specs=(vmem, vmem),
        scratch_shapes=[
            pltpu.VMEM((cap, BLOCK, BLOCK), BF),
            pltpu.VMEM((ITERS, n_date, ru, rank), BF),
            pltpu.VMEM((ITERS, n_pix, rv, rank), BF),
            pltpu.VMEM((ITERS, n_date, ru, rank), BF),
            pltpu.VMEM((ITERS, n_date, ru, rank), BF),
            pltpu.VMEM((ITERS, n_pix, rv, rank), BF),
            pltpu.VMEM((ITERS, n_pix, rv, rank), BF),
            pltpu.VMEM((cols, rank), BF),
            pltpu.VMEM((ru, cols), BF),
            pltpu.VMEM((rank, cols), F32),
            pltpu.VMEM((ru, rank), BF),
            dma,
            dma((ITERS, n_date)), dma((ITERS, n_date)),
            dma((ITERS, n_pix)), dma((ITERS, n_pix)),
            dma((ITERS, n_date)), dma((ITERS, n_date)),
            dma((ITERS, n_pix)), dma((ITERS, n_pix)),
        ],
        compiler_params=pltpu.CompilerParams(
            collective_id=0, has_side_effects=True, vmem_limit_bytes=48 * 1024 * 1024
        ),
    )(slot, live, pixel_factor, date_factor, clear_obs.reshape(cap, BLOCK, BLOCK))


def solution(mesh):
    in_specs = (
        P(("pix", "date"), None),
        P(("date", "pix"), None),
        P("pix", "date", None, None, None),
        P("pix", "date", None),
        P("pix", "date"),
    )
    out_specs = (P(("pix", "date"), None), P(("date", "pix"), None))
    body = functools.partial(shards, mesh.shape["pix"], mesh.shape["date"])
    return jax.shard_map(body, mesh=mesh, in_specs=in_specs, out_specs=out_specs, check_vma=False)
```

time: 229 us -> 71.2 us (0.31)
  waiting for transfers between devices: 112 us -> 0 us
  Pallas kernels: 0 us -> 64.2 us
  other arithmetic: 39.1 us -> 0.19 us
  blocking collectives: 30.7 us -> 0 us
  matrix products: 21.5 us -> 0 us
  between operations: 14.9 us -> 1.31 us
  local copies, waits for them, and re-layouts: 9.85 us -> 5.24 us
    reduce_scatter x4 -> x0, waiting for transfers between devices: 92.5 us -> none  [the longest x2 49.9 us: shards(): lax.psum_scatter(date_grad.astype(jnp.bfloat16), 'pix', scatter_dimension...]
    pallas_call x0 -> x1, Pallas kernels: none -> 64.2 us  [shards(): pl.pallas_call(body, out_shape=(jax.ShapeDtypeStruct((ru, rank), F32), ja...]
    all_gather x2 -> x0, blocking collectives: 30.7 us -> none  [shards(): lax.all_gather(date_now.astype(jnp.bfloat16), 'pix', axis=0, tiled=True)]
    scatter-add x4 -> x0, other arithmetic: 26 us -> none  [the longest x2 13 us: block_terms(): jnp.zeros((col_blocks, BLOCK, rank_width), jnp.float32).at[col_index]]
    dot_general x6 -> x0, matrix products: 21.5 us -> none  [the longest x2 8 us: block_terms(): jnp.einsum('kij,kir->kjr', misfit, pixel_tiles, preferred_element_type=jn...]
    all_gather x2 -> x0, waiting for transfers between devices: 19.5 us -> none  [shards(): lax.all_gather(pixel_now.astype(jnp.bfloat16), 'date', axis=0, tiled=True)]
    gather x4 -> x0, local copies, waits for them, and re-layouts: 9.18 us -> none  [the longest x2 5.16 us: block_terms(): pixel_tiles = pixel_panel.reshape(row_blocks, BLOCK, rank_width)[row_index]]
    convert_element_type x8 -> x0, other arithmetic: 9.07 us -> none  [the longest x2 3.5 us: shards(): pixel_now.astype(jnp.bfloat16)]
  transfers between devices with their start and end apart: 6 -> 0, of which waited for: 6 -> 0; matrix products, arithmetic and copies ran while one was open for 15% -> 0% of each run, Pallas kernels for 0% -> 0%
where the time goes in v1:
time: 71.2 us; the launch traced here: 71 us
  Pallas kernels  64.2 us (90%)
  local copies, waits for them, and re-layouts  5.24 us (7%)
  between operations  1.31 us (2%)
    pallas_call x1, Pallas kernels, shards(): pl.pallas_call(body, out_shape=(jax.ShapeDtypeStruct((ru, rank), F32), ja...  64.2 us
    unnamed x10, local copies, waits for them, and re-layouts  5.24 us

profile of v1, /device:TPU:0, one launch (start us, length us, event | category | flops | bytes accessed | tf_op | source)
XLA Modules:
  0.0 71.0 jit_solution(3284599770654698919)
XLA Ops:
  1.3 0.0 copy-start.3
  1.3 0.6 copy-done.3
  1.9 0.1 convert_reduce_fusion.live_ref
  2.0 0.1 select_reduce_fusion.slot_ref
  2.1 0.0 copy-start
  2.1 1.2 %copy-done = bf16[1,1,32,128,128]{4,3,2,1,0:T(8,128)(2,1)S(1)} copy-done((bf16[1,1,32,128,128]{4,3,2,1,0:T(8,128)(2,1)S(1)}, bf16[1,1,32,128,128]{4,3,2,1,0:T(8,128)(2,1)}, u32[]{:S(2)}) %copy-start) | copy-done | bytes 1048600
  3.4 0.0 copy-start.1
  3.4 1.0 %copy-done.1 = f32[512,256]{1,0:T(8,128)S(1)} copy-done((f32[512,256]{1,0:T(8,128)S(1)}, f32[512,256]{1,0:T(8,128)}, u32[]{:S(2)}) %copy-start.1) | copy-done | bytes 524312
  4.4 0.0 copy-start.2
  4.4 0.9 %copy-done.2 = f32[96,256]{1,0:T(8,128)S(1)} copy-done((f32[96,256]{1,0:T(8,128)S(1)}, f32[96,256]{1,0:T(8,128)}, u32[]{:S(2)}) %copy-start.2) | copy-done | bytes 98328
  5.3 64.2 %shard_map.68 = (f32[512,256]{1,0:T(8,128)S(1)}, f32[96,256]{1,0:T(8,128)S(1)}) custom-call(s32[96]{0:T(128)S(1)} %select_reduce_fusion.slot_ref, f32[96]{0:T(128)S(1)} %convert_reduce_fusion.live_ref, f32[512,256]{1,0:T(8,128)S(1)} %copy-done.1, f32[96,256]{1,0:T(8,128)S(1)} %copy-done.2, bf16[32,128,128]{2,1,0:T(8,128)(2,1)S(1)} %bitcast.4), custom_call_target="tpu_custom_call" | custom-call | tf_op jit(solution)/shard_map/pallas_call | solution.py:167
  69.5 0.8 %copy.10 = f32[512,256]{1,0:T(8,128)} copy(f32[512,256]{1,0:T(8,128)S(1)} %get-tuple-element.4) | data formatting | bytes 1048576
  70.3 0.6 copy.11
  (1 shorter events, 0.0 us)
Async XLA Ops:
  1.3 0.7 copy-start.3
  2.1 1.2 %copy-start = (bf16[1,1,32,128,128]{4,3,2,1,0:T(8,128)(2,1)S(1)}, bf16[1,1,32,128,128]{4,3,2,1,0:T(8,128)(2,1)}, u32[]{:S(2)}) copy-start(bf16[1,1,32,128,128]{4,3,2,1,0:T(8,128)(2,1)} %param.7) | copy-start | bytes 3145732
  3.4 1.0 %copy-start.1 = (f32[512,256]{1,0:T(8,128)S(1)}, f32[512,256]{1,0:T(8,128)}, u32[]{:S(2)}) copy-start(f32[512,256]{1,0:T(8,128)} %u_ref.1) | copy-start | bytes 1572868
  4.4 0.9 %copy-start.2 = (f32[96,256]{1,0:T(8,128)S(1)}, f32[96,256]{1,0:T(8,128)}, u32[]{:S(2)}) copy-start(f32[96,256]{1,0:T(8,128)} %v_ref.1) | copy-start | bytes 294916

commit v2 on v1

v2 whole, which is shorter than its diff:
```python
import functools

import jax
import jax.numpy as jnp
from jax import lax
from jax.experimental import pallas as pl
from jax.experimental.pallas import tpu as pltpu
from jax.sharding import PartitionSpec as P

BLOCK = 128
ITERS = 2
MESH = pl.DeviceIdType.MESH
BF = jnp.bfloat16
F32 = jnp.float32


def dot(a, b, ca, cb):
    return lax.dot_general(a, b, (((ca,), (cb,)), ((), ())), preferred_element_type=F32)


def kernel(
    n_pix, n_date, rate_u, rate_v,
    slot_ref, live_ref, u_hbm, v_hbm, obs_hbm, u_out, v_out,
    u_ref, v_ref, obs, ubuf, vbuf, gus, gur, gvf, gvs, gvr, gve, gvo, vpan, mbuf, gvt, own_gu, keep,
    load_sem, us, ur, vs, vr, ws, wr, gu_s, gu_r, gv_s, gv_r, ge_s, ge_r,
):
    me_p = lax.axis_index("pix")
    me_d = lax.axis_index("date")
    ru, rank = u_ref.shape
    rv = v_ref.shape[0]
    cols = n_pix * rv
    cb = cols // BLOCK
    chips = n_pix // 2
    square = n_date == 4 and ru % (2 * BLOCK) == 0
    half = ru // 2
    piece = mbuf.shape[0]
    nb = piece // BLOCK

    load_u = pltpu.make_async_copy(u_hbm, u_ref, load_sem.at[0])
    load_v = pltpu.make_async_copy(v_hbm, v_ref, load_sem.at[1])
    load_o = pltpu.make_async_copy(obs_hbm, obs, load_sem.at[2])
    load_u.start()
    load_v.start()
    load_o.start()

    core = lax.rem(me_p, 2)
    sib = me_p + 1 - 2 * core

    def at_date(s):
        return lax.rem(me_d + s, n_date)

    def at_chip(k):
        return lax.rem(me_p + 2 * k, n_pix)

    xn = me_d + 1 - 2 * lax.rem(me_d, 2)
    yn = lax.rem(me_d + 2, n_date)
    diag = lax.rem(xn + 2, n_date)

    def copy(src, dst, ssem, rsem, p, d):
        return pltpu.make_async_remote_copy(
            src_ref=src, dst_ref=dst, send_sem=ssem, recv_sem=rsem, device_id=(p, d), device_id_type=MESH
        )

    def v_copy(t, k):
        return copy(vbuf.at[t, me_p], vbuf.at[t, me_p], vs.at[t, k], vr.at[t, k], at_chip(k), me_d)

    def v_pass(t, k):
        held = vbuf.at[t, at_chip(chips - k)]
        return copy(held, held, ws.at[t, k], wr.at[t, k], sib, me_d)

    def ge_copy(t):
        return copy(gve.at[t], gvo.at[t], ge_s.at[t], ge_r.at[t], sib, me_d)

    def gv_copy(t, k):
        return copy(gvs.at[t, k], gvr.at[t, k], gv_s.at[t, k], gv_r.at[t, k], at_chip(k), me_d)

    def u_copy(t, s):
        return copy(ubuf.at[t, me_d], ubuf.at[t, me_d], us.at[t, s], ur.at[t, s], me_p, at_date(s))

    def gu_copy(t, s):
        return copy(gus.at[t, s], gur.at[t, s], gu_s.at[t, s], gu_r.at[t, s], me_p, at_date(s))

    def u_square(t, i):
        owner, h, to = (
            (me_d, 0, xn), (me_d, 1, yn), (me_d, 1, xn), (me_d, 0, yn), (xn, 0, yn), (yn, 1, xn),
        )[i]
        part = ubuf.at[t, owner, pl.ds(h * half, half)]
        return copy(part, part, us.at[t, i], ur.at[t, i], me_p, to)

    def gu_square(t, i):
        to = xn if i in (0, 2, 5) else yn
        return copy(gus.at[t, i], gur.at[t, i], gu_s.at[t, i], gu_r.at[t, i], me_p, to)

    barrier = pltpu.get_barrier_semaphore()

    def greet(p, d):
        pl.semaphore_signal(barrier, inc=1, device_id=(p, d), device_id_type=MESH)

    greet(sib, me_d)
    for k in range(1, chips):
        greet(at_chip(k), me_d)
    if square:
        greet(me_p, xn)
        greet(me_p, yn)
    else:
        for s in range(1, n_date):
            greet(me_p, at_date(s))
    load_u.wait()
    ubuf[0, me_d] = u_ref[...].astype(BF)
    load_v.wait()
    vbuf[0, me_p] = v_ref[...].astype(BF)
    pl.semaphore_wait(barrier, chips + (2 if square else n_date - 1))

    def tile(t, source, start):
        uc = ubuf.at[t, source, pl.ds(start, piece)]
        base = source * (ru // BLOCK) + start // BLOCK

        def rows(ib, carry):
            first = pl.multiple_of(ib * BLOCK, BLOCK)
            predicted = dot(uc[pl.ds(first, BLOCK), :], vpan[...], 1, 1)
            for j in range(cb):
                b = (base + ib) * cb + j
                o = obs[slot_ref[b]].astype(F32)
                m = (predicted[:, j * BLOCK:(j + 1) * BLOCK] - o) * live_ref[b]
                mbuf[pl.ds(first, BLOCK), j * BLOCK:(j + 1) * BLOCK] = m.astype(BF)
            return carry

        lax.fori_loop(0, nb, rows, 0)
        misfit = mbuf[...]
        return dot(misfit, vpan[...], 1, 0), dot(uc[...], misfit, 0, 0)

    def date_start(t):
        for k in range(1, chips):
            v_copy(t, k).start()
        v_pass(t, 0).start()

    def date_pass(t):
        for k in range(1, chips):
            v_copy(t, k).wait_recv()
            v_pass(t, k).start()

    def date_panel(t):
        for k in range(chips):
            v_pass(t, k).wait_recv()
        panel = vbuf[t]
        if rv % 16:
            panel = panel.astype(F32)
        vpan[...] = panel.reshape(cols, rank).astype(BF)

    def pixel_pass(t):
        u_square(t, 0).wait_recv()
        u_square(t, 4).start()
        u_square(t, 1).wait_recv()
        u_square(t, 5).start()

    def date_grad_send(t):
        gvf[...] = gvt[...].T.reshape(n_pix, rv, rank)
        for k in range(chips):
            gve[t, k] = gvf[2 * k + 1 - core].astype(BF)
        ge_copy(t).start()

    def date_grad_pass(t):
        ge_copy(t).wait_recv()
        chip = me_p // 2
        for k in range(1, chips):
            to = lax.rem(chip + k, chips)
            gvs[t, k] = (gvf[2 * to + core] + gvo[t, to].astype(F32)).astype(BF)
            gv_copy(t, k).start()

    def date_update(t, v_prev):
        total = gvf[me_p] + gvo[t, me_p // 2].astype(F32)
        for k in range(1, chips):
            gv_copy(t, k).wait_recv()
            total += gvr[t, k].astype(F32)
        v_out[...] = v_prev[...] - rate_v * total
        if t + 1 < ITERS:
            vbuf[t + 1, me_p] = v_out[...].astype(BF)
            date_start(t + 1)

    u_prev, v_prev = u_ref, v_ref
    if square:
        u_square(0, 0).start()
        u_square(0, 1).start()
    date_start(0)
    if square:
        u_square(0, 2).start()
        u_square(0, 3).start()
    for t in range(ITERS):
        if not square:
            for s in range(1, n_date):
                u_copy(t, s).start()
        elif t == 0:
            pixel_pass(t)
        date_pass(t)
        if square and t > 0:
            pixel_pass(t)
        date_panel(t)
        if t == 0:
            load_o.wait()
        gvt[...] = jnp.zeros_like(gvt)

        if square:
            for i, source, h in (
                (None, me_d, 0), (None, me_d, 1), (0, xn, 0), (1, yn, 1),
                (2, xn, 1), (3, yn, 0), (4, diag, 0), (5, diag, 1),
            ):
                if i is not None:
                    if i > 1:
                        u_square(t, i).wait_recv()
                gu, gv = tile(t, source, h * half)
                gvt[...] += gv
                if i is None:
                    own_gu[h * half:(h + 1) * half, :] = gu
                elif i in (2, 3):
                    keep[i - 2] = gu
                else:
                    j = i if i < 2 else i - 2
                    gus[t, j] = gu.astype(BF)
                    gu_square(t, j).start()
        else:
            gu, gv = tile(t, me_d, 0)
            own_gu[...] = gu
            gvt[...] += gv

            def step(s, carry):
                u_copy(t, n_date - s).wait_recv()
                gu, gv = tile(t, at_date(s), 0)
                gus[t, s] = gu.astype(BF)
                gvt[...] += gv
                gu_copy(t, s).start()
                return carry

            lax.fori_loop(1, n_date, step, 0)

        date_grad_send(t)
        date_grad_pass(t)
        if square:
            for i, kept in ((4, 1), (5, 0)):
                gu_square(t, i - 2).wait_recv()
                gus[t, i] = (keep[kept] + gur[t, i - 2].astype(F32)).astype(BF)
                gu_square(t, i).start()
        date_update(t, v_prev)
        if square:
            for h in range(2):
                rows = slice(h * half, (h + 1) * half)
                gu_square(t, h).wait_recv()
                gu_square(t, 4 + h).wait_recv()
                total = own_gu[rows, :] + gur[t, h].astype(F32) + gur[t, 4 + h].astype(F32)
                u_out[rows, :] = u_prev[rows, :] - rate_u * total
                if t + 1 < ITERS:
                    ubuf[t + 1, me_d, rows, :] = u_out[rows, :].astype(BF)
                    for i in ((0, 3), (1, 2))[h]:
                        u_square(t + 1, i).start()
        else:
            total = own_gu[...]
            for s in range(1, n_date):
                gu_copy(t, s).wait_recv()
                total += gur[t, s].astype(F32)
            u_out[...] = u_prev[...] - rate_u * total
            if t + 1 < ITERS:
                ubuf[t + 1, me_d] = u_out[...].astype(BF)
        u_prev, v_prev = u_out, v_out

    for t in range(ITERS):
        ge_copy(t).wait_send()
        for k in range(chips):
            v_pass(t, k).wait_send()
        for k in range(1, chips):
            v_copy(t, k).wait_send()
            gv_copy(t, k).wait_send()
        if square:
            for i in range(6):
                u_square(t, i).wait_send()
                gu_square(t, i).wait_send()
        else:
            for s in range(1, n_date):
                u_copy(t, s).wait_send()
                gu_copy(t, s).wait_send()


def shards(n_pix, n_date, pixel_factor, date_factor, clear_obs, clear_blocks, clear_count):
    ru, rank = pixel_factor.shape
    rv = date_factor.shape[0]
    devices = n_pix * n_date
    cap = clear_obs.shape[2]
    cols = n_pix * rv
    blocks_in_tile = (n_date * ru // BLOCK) * (cols // BLOCK)
    match = (clear_blocks[0, 0][None, :] == jnp.arange(blocks_in_tile)[:, None]) & (
        jnp.arange(cap)[None, :] < clear_count[0, 0]
    )
    slot = jnp.sum(jnp.where(match, jnp.arange(cap)[None, :], 0), axis=1).astype(jnp.int32)
    live = jnp.sum(match.astype(F32), axis=1)
    body = functools.partial(
        kernel, n_pix, n_date, 64.0 / (rv * devices), 64.0 / (ru * devices)
    )
    chips = n_pix // 2
    square = n_date == 4 and ru % (2 * BLOCK) == 0
    piece = ru // 2 if square else ru
    parts = 6 if square else n_date
    vmem = pl.BlockSpec(memory_space=pltpu.VMEM)
    smem = pl.BlockSpec(memory_space=pltpu.SMEM)
    hbm = pl.BlockSpec(memory_space=pl.ANY)
    dma = pltpu.SemaphoreType.DMA
    return pl.pallas_call(
        body,
        out_shape=(
            jax.ShapeDtypeStruct((ru, rank), F32),
            jax.ShapeDtypeStruct((rv, rank), F32),
        ),
        in_specs=[smem, smem, hbm, hbm, hbm],
        out_specs=(vmem, vmem),
        scratch_shapes=[
            pltpu.VMEM((ru, rank), F32),
            pltpu.VMEM((rv, rank), F32),
            pltpu.VMEM((cap, BLOCK, BLOCK), BF),
            pltpu.VMEM((ITERS, n_date, ru, rank), BF),
            pltpu.VMEM((ITERS, n_pix, rv, rank), BF),
            pltpu.VMEM((ITERS, parts, piece, rank), BF),
            pltpu.VMEM((ITERS, parts, piece, rank), BF),
            pltpu.VMEM((n_pix, rv, rank), F32),
            pltpu.VMEM((ITERS, chips, rv, rank), BF),
            pltpu.VMEM((ITERS, chips, rv, rank), BF),
            pltpu.VMEM((ITERS, chips, rv, rank), BF),
            pltpu.VMEM((ITERS, chips, rv, rank), BF),
            pltpu.VMEM((cols, rank), BF),
            pltpu.VMEM((piece, cols), BF),
            pltpu.VMEM((rank, cols), F32),
            pltpu.VMEM((ru, rank), F32),
            pltpu.VMEM((2, piece, rank), F32),
            dma((3,)),
            dma((ITERS, parts)), dma((ITERS, parts)),
            dma((ITERS, chips)), dma((ITERS, chips)),
            dma((ITERS, chips)), dma((ITERS, chips)),
            dma((ITERS, parts)), dma((ITERS, parts)),
            dma((ITERS, chips)), dma((ITERS, chips)),
            dma((ITERS,)), dma((ITERS,)),
        ],
        compiler_params=pltpu.CompilerParams(
            collective_id=0, has_side_effects=True, vmem_limit_bytes=60 * 1024 * 1024
        ),
    )(slot, live, pixel_factor, date_factor, clear_obs.reshape(cap, BLOCK, BLOCK))


def solution(mesh):
    in_specs = (
        P(("pix", "date"), None),
        P(("date", "pix"), None),
        P("pix", "date", None, None, None),
        P("pix", "date", None),
        P("pix", "date"),
    )
    out_specs = (P(("pix", "date"), None), P(("date", "pix"), None))
    body = functools.partial(shards, mesh.shape["pix"], mesh.shape["date"])
    return jax.shard_map(body, mesh=mesh, in_specs=in_specs, out_specs=out_specs, check_vma=False)
```

time: 71.2 us -> 61 us (0.86)
  Pallas kernels: 64.2 us -> 55.1 us
  local copies, waits for them, and re-layouts: 5.24 us -> 3.2 us
  other arithmetic: 0.19 us -> 1.21 us
    pallas_call x1, Pallas kernels: 64.2 us -> 55.1 us  [shards(): pl.pallas_call(body, out_shape=(jax.ShapeDtypeStruct((ru, rank), F32), ja...]
    unnamed x10 -> x6, local copies, waits for them, and re-layouts: 5.24 us -> 3.2 us
where the time goes in v2:
time: 61 us; the launch traced here: 60.8 us
  Pallas kernels  55.1 us (90%)
  local copies, waits for them, and re-layouts  3.2 us (5%)
  between operations  1.31 us (2%)
  other arithmetic  1.21 us (2%)
    pallas_call x1, Pallas kernels, shards(): pl.pallas_call(body, out_shape=(jax.ShapeDtypeStruct((ru, rank), F32), ja...  55.1 us
    unnamed x6, local copies, waits for them, and re-layouts  3.2 us

profile of v2, /device:TPU:0, one launch (start us, length us, event | category | flops | bytes accessed | tf_op | source)
XLA Modules:
  0.0 60.8 jit_solution(14985401735872053911)
XLA Ops:
  1.3 0.0 copy-start.1
  1.3 0.6 %copy-done.1 = s32[1,1,32]{2,1,0:T(1,128)S(1)} copy-done((s32[1,1,32]{2,1,0:T(1,128)S(1)}, s32[1,1,32]{2,1,0:T(1,128)}, u32[]{:S(2)}) %copy-start.1) | copy-done | bytes 152
  1.9 0.6 convert_reduce_fusion.live_ref
  2.6 0.6 select_reduce_fusion.slot_ref
  3.2 55.1 %shard_map.68 = (f32[512,256]{1,0:T(8,128)}, f32[96,256]{1,0:T(8,128)}) custom-call(s32[96]{0:T(128)} %select_reduce_fusion.slot_ref, f32[96]{0:T(128)} %convert_reduce_fusion.live_ref, f32[512,256]{1,0:T(8,128)} %u_hbm.1, f32[96,256]{1,0:T(8,128)} %v_hbm.1, bf16[32,128,128]{2,1,0:T(8,128)(2,1)} %bitcast.4), custom_call_target="tpu_custom_call" | custom-call | tf_op jit(solution)/shard_map/pallas_call | solution.py:304
  58.3 0.0 copy-start
  58.3 1.9 %copy.10 = f32[512,256]{1,0:T(8,128)} copy(f32[512,256]{1,0:T(8,128)} %get-tuple-element.4) | data formatting | bytes 1048576
  60.2 0.0 copy-done
  60.2 0.6 %copy.11 = f32[96,256]{1,0:T(8,128)} copy(f32[96,256]{1,0:T(8,128)S(1)} %copy-done) | data formatting | bytes 196608
  (1 shorter events, 0.0 us)
Async XLA Ops:
  1.3 0.7 %copy-start.1 = (s32[1,1,32]{2,1,0:T(1,128)S(1)}, s32[1,1,32]{2,1,0:T(1,128)}, u32[]{:S(2)}) copy-start(s32[1,1,32]{2,1,0:T(1,128)} %param.8) | copy-start | bytes 388
  58.3 1.9 %copy-start = (f32[96,256]{1,0:T(8,128)S(1)}, f32[96,256]{1,0:T(8,128)}, u32[]{:S(2)}) copy-start(f32[96,256]{1,0:T(8,128)} %get-tuple-element.5) | copy-start | bytes 294916

commit v3 on v2

--- a/solution.py
+++ b/solution.py
@@ -20,8 +20,8 @@
 
 def kernel(
     n_pix, n_date, rate_u, rate_v,
-    slot_ref, live_ref, u_hbm, v_hbm, obs_hbm, u_out, v_out,
-    u_ref, v_ref, obs, ubuf, vbuf, gus, gur, gvf, gvs, gvr, gve, gvo, vpan, mbuf, gvt, own_gu, keep,
+    table_ref, u_hbm, v_hbm, obs_hbm, u_out, v_out,
+    u_ref, v_ref, obs, ubuf, vbuf, gus, gur, gvf, gvs, gvr, gve, gvo, vpan, vpant, mbuf, gvt, own_gu, keep,
     load_sem, us, ur, vs, vr, ws, wr, gu_s, gu_r, gv_s, gv_r, ge_s, ge_r,
 ):
     me_p = lax.axis_index("pix")
@@ -115,17 +115,14 @@
         uc = ubuf.at[t, source, pl.ds(start, piece)]
         base = source * (ru // BLOCK) + start // BLOCK
 
-        def rows(ib, carry):
-            first = pl.multiple_of(ib * BLOCK, BLOCK)
-            predicted = dot(uc[pl.ds(first, BLOCK), :], vpan[...], 1, 1)
+        predicted = dot(uc[...], vpant[...], 1, 0)
+        for ib in range(nb):
             for j in range(cb):
-                b = (base + ib) * cb + j
-                o = obs[slot_ref[b]].astype(F32)
-                m = (predicted[:, j * BLOCK:(j + 1) * BLOCK] - o) * live_ref[b]
-                mbuf[pl.ds(first, BLOCK), j * BLOCK:(j + 1) * BLOCK] = m.astype(BF)
-            return carry
-
-        lax.fori_loop(0, nb, rows, 0)
+                code = table_ref[(base + ib) * cb + j]
+                o = obs[jnp.maximum(code, 0)].astype(F32)
+                here = (slice(ib * BLOCK, (ib + 1) * BLOCK), slice(j * BLOCK, (j + 1) * BLOCK))
+                m = (predicted[here] - o) * jnp.where(code >= 0, 1.0, 0.0)
+                mbuf[here] = m.astype(BF)
         misfit = mbuf[...]
         return dot(misfit, vpan[...], 1, 0), dot(uc[...], misfit, 0, 0)
 
@@ -146,6 +143,7 @@
         if rv % 16:
             panel = panel.astype(F32)
         vpan[...] = panel.reshape(cols, rank).astype(BF)
+        vpant[...] = vpan[...].T
 
     def pixel_pass(t):
         u_square(t, 0).wait_recv()
@@ -201,8 +199,8 @@
 
         if square:
             for i, source, h in (
-                (None, me_d, 0), (None, me_d, 1), (0, xn, 0), (1, yn, 1),
-                (2, xn, 1), (3, yn, 0), (4, diag, 0), (5, diag, 1),
+                (0, xn, 0), (1, yn, 1), (4, diag, 0), (5, diag, 1),
+                (2, xn, 1), (3, yn, 0), (None, me_d, 0), (None, me_d, 1),
             ):
                 if i is not None:
                     if i > 1:
@@ -211,6 +209,9 @@
                 gvt[...] += gv
                 if i is None:
                     own_gu[h * half:(h + 1) * half, :] = gu
+                    gu_square(t, 2 + h).wait_recv()
+                    gus[t, 4 + h] = (keep[1 - h] + gur[t, 2 + h].astype(F32)).astype(BF)
+                    gu_square(t, 4 + h).start()
                 elif i in (2, 3):
                     keep[i - 2] = gu
                 else:
@@ -234,11 +235,6 @@
 
         date_grad_send(t)
         date_grad_pass(t)
-        if square:
-            for i, kept in ((4, 1), (5, 0)):
-                gu_square(t, i - 2).wait_recv()
-                gus[t, i] = (keep[kept] + gur[t, i - 2].astype(F32)).astype(BF)
-                gu_square(t, i).start()
         date_update(t, v_prev)
         if square:
             for h in range(2):
@@ -288,8 +284,7 @@
     match = (clear_blocks[0, 0][None, :] == jnp.arange(blocks_in_tile)[:, None]) & (
         jnp.arange(cap)[None, :] < clear_count[0, 0]
     )
-    slot = jnp.sum(jnp.where(match, jnp.arange(cap)[None, :], 0), axis=1).astype(jnp.int32)
-    live = jnp.sum(match.astype(F32), axis=1)
+    table = jnp.max(jnp.where(match, jnp.arange(cap)[None, :], -1), axis=1).astype(jnp.int32)
     body = functools.partial(
         kernel, n_pix, n_date, 64.0 / (rv * devices), 64.0 / (ru * devices)
     )
@@ -307,7 +302,7 @@
             jax.ShapeDtypeStruct((ru, rank), F32),
             jax.ShapeDtypeStruct((rv, rank), F32),
         ),
-        in_specs=[smem, smem, hbm, hbm, hbm],
+        in_specs=[smem, hbm, hbm, hbm],
         out_specs=(vmem, vmem),
         scratch_shapes=[
             pltpu.VMEM((ru, rank), F32),
@@ -323,6 +318,7 @@
             pltpu.VMEM((ITERS, chips, rv, rank), BF),
             pltpu.VMEM((ITERS, chips, rv, rank), BF),
             pltpu.VMEM((cols, rank), BF),
+            pltpu.VMEM((rank, cols), BF),
             pltpu.VMEM((piece, cols), BF),
             pltpu.VMEM((rank, cols), F32),
             pltpu.VMEM((ru, rank), F32),
@@ -338,7 +334,7 @@
         compiler_params=pltpu.CompilerParams(
             collective_id=0, has_side_effects=True, vmem_limit_bytes=60 * 1024 * 1024
         ),
-    )(slot, live, pixel_factor, date_factor, clear_obs.reshape(cap, BLOCK, BLOCK))
+    )(table, pixel_factor, date_factor, clear_obs.reshape(cap, BLOCK, BLOCK))
 
 
 def solution(mesh):

time: 61 us -> 60.2 us (0.987); the launches traced: 60.8 us -> 59.4 us
  Pallas kernels: 55.1 us -> 54.3 us
    reduce_sum x2 -> x0, other arithmetic: 1.21 us -> none  [the longest x1 0.6 us: shards(): live = jnp.sum(match.astype(F32), axis=1)]
    pallas_call x1, Pallas kernels: 55.1 us -> 54.3 us  [shards(): pl.pallas_call(body, out_shape=(jax.ShapeDtypeStruct((ru, rank), F32), ja...]
where the time goes in v3:
time: 60.2 us; the launch traced here: 59.4 us
  Pallas kernels  54.3 us (90%)
  local copies, waits for them, and re-layouts  3.2 us (5%)
  between operations  1.31 us (2%)
  other arithmetic  0.61 us (1%)
    pallas_call x1, Pallas kernels, shards(): pl.pallas_call(body, out_shape=(jax.ShapeDtypeStruct((ru, rank), F32), ja...  54.3 us
    unnamed x6, local copies, waits for them, and re-layouts  3.2 us

profile of v3, /device:TPU:0, one launch (start us, length us, event | category | flops | bytes accessed | tf_op | source)
XLA Modules:
  0.0 59.4 jit_solution(9799653605370717653)
XLA Ops:
  1.3 0.0 copy-start.1
  1.3 0.6 %copy-done.1 = s32[1,1,32]{2,1,0:T(1,128)S(1)} copy-done((s32[1,1,32]{2,1,0:T(1,128)S(1)}, s32[1,1,32]{2,1,0:T(1,128)}, u32[]{:S(2)}) %copy-start.1) | copy-done | bytes 152
  1.9 0.6 %select_reduce_fusion.table_ref = s32[96]{0:T(128)} fusion(s32[32]{0:T(128)S(1)} %bitcast.5, pred[32]{0:T(512)(128)(4,1)S(1)} %iota_compare_fusion.1), kind=kLoop, calls=%fused_computation | loop fusion | flops 12192 | bytes 544 | tf_op jit(solution)/shard_map/reduce_max | solution.py:287
  2.6 54.3 %shard_map.68 = (f32[512,256]{1,0:T(8,128)}, f32[96,256]{1,0:T(8,128)}) custom-call(s32[96]{0:T(128)} %select_reduce_fusion.table_ref, f32[512,256]{1,0:T(8,128)} %u_hbm.1, f32[96,256]{1,0:T(8,128)} %v_hbm.1, bf16[32,128,128]{2,1,0:T(8,128)(2,1)} %bitcast.4), custom_call_target="tpu_custom_call" | custom-call | tf_op jit(solution)/shard_map/pallas_call | solution.py:299
  56.8 0.0 copy-start
  56.9 1.9 %copy.10 = f32[512,256]{1,0:T(8,128)} copy(f32[512,256]{1,0:T(8,128)} %get-tuple-element.4) | data formatting | bytes 1048576
  58.8 0.0 copy-done
  58.8 0.6 %copy.11 = f32[96,256]{1,0:T(8,128)} copy(f32[96,256]{1,0:T(8,128)S(1)} %copy-done) | data formatting | bytes 196608
  (1 shorter events, 0.0 us)
Async XLA Ops:
  1.3 0.7 %copy-start.1 = (s32[1,1,32]{2,1,0:T(1,128)S(1)}, s32[1,1,32]{2,1,0:T(1,128)}, u32[]{:S(2)}) copy-start(s32[1,1,32]{2,1,0:T(1,128)} %param.8) | copy-start | bytes 388
  56.8 1.9 %copy-start = (f32[96,256]{1,0:T(8,128)S(1)}, f32[96,256]{1,0:T(8,128)}, u32[]{:S(2)}) copy-start(f32[96,256]{1,0:T(8,128)} %get-tuple-element.5) | copy-start | bytes 294916

commit v4 on v3

--- a/solution.py
+++ b/solution.py
@@ -187,11 +187,9 @@
         if not square:
             for s in range(1, n_date):
                 u_copy(t, s).start()
-        elif t == 0:
+        else:
             pixel_pass(t)
         date_pass(t)
-        if square and t > 0:
-            pixel_pass(t)
         date_panel(t)
         if t == 0:
             load_o.wait()
@@ -235,7 +233,6 @@
 
         date_grad_send(t)
         date_grad_pass(t)
-        date_update(t, v_prev)
         if square:
             for h in range(2):
                 rows = slice(h * half, (h + 1) * half)
@@ -255,6 +252,7 @@
             u_out[...] = u_prev[...] - rate_u * total
             if t + 1 < ITERS:
                 ubuf[t + 1, me_d] = u_out[...].astype(BF)
+        date_update(t, v_prev)
         u_prev, v_prev = u_out, v_out
 
     for t in range(ITERS):

time: 60.2 us -> 59.4 us (0.987); the launches traced: 59.4 us -> 59.3 us
  no operation moved by 1% of the time
where the time goes in v4:
time: 59.4 us; the launch traced here: 59.3 us
  Pallas kernels  54.1 us (91%)
  local copies, waits for them, and re-layouts  3.2 us (5%)
  between operations  1.31 us (2%)
  other arithmetic  0.61 us (1%)
    pallas_call x1, Pallas kernels, shards(): pl.pallas_call(body, out_shape=(jax.ShapeDtypeStruct((ru, rank), F32), ja...  54.1 us
    unnamed x6, local copies, waits for them, and re-layouts  3.2 us

profile of v4, /device:TPU:0, one launch (start us, length us, event | category | flops | bytes accessed | tf_op | source)
XLA Modules:
  0.0 59.3 jit_solution(17382453603040396952)
XLA Ops:
  1.3 0.0 copy-start.1
  1.3 0.6 %copy-done.1 = s32[1,1,32]{2,1,0:T(1,128)S(1)} copy-done((s32[1,1,32]{2,1,0:T(1,128)S(1)}, s32[1,1,32]{2,1,0:T(1,128)}, u32[]{:S(2)}) %copy-start.1) | copy-done | bytes 152
  1.9 0.6 %select_reduce_fusion.table_ref = s32[96]{0:T(128)} fusion(s32[32]{0:T(128)S(1)} %bitcast.5, pred[32]{0:T(512)(128)(4,1)S(1)} %iota_compare_fusion.1), kind=kLoop, calls=%fused_computation | loop fusion | flops 12192 | bytes 544 | tf_op jit(solution)/shard_map/reduce_max | solution.py:285
  2.6 54.1 %shard_map.68 = (f32[512,256]{1,0:T(8,128)}, f32[96,256]{1,0:T(8,128)}) custom-call(s32[96]{0:T(128)} %select_reduce_fusion.table_ref, f32[512,256]{1,0:T(8,128)} %u_hbm.1, f32[96,256]{1,0:T(8,128)} %v_hbm.1, bf16[32,128,128]{2,1,0:T(8,128)(2,1)} %bitcast.4), custom_call_target="tpu_custom_call" | custom-call | tf_op jit(solution)/shard_map/pallas_call | solution.py:297
  56.7 0.0 copy-start
  56.7 1.9 %copy.10 = f32[512,256]{1,0:T(8,128)} copy(f32[512,256]{1,0:T(8,128)} %get-tuple-element.4) | data formatting | bytes 1048576
  58.6 0.0 copy-done
  58.6 0.6 %copy.11 = f32[96,256]{1,0:T(8,128)} copy(f32[96,256]{1,0:T(8,128)S(1)} %copy-done) | data formatting | bytes 196608
  (1 shorter events, 0.0 us)
Async XLA Ops:
  1.3 0.7 %copy-start.1 = (s32[1,1,32]{2,1,0:T(1,128)S(1)}, s32[1,1,32]{2,1,0:T(1,128)}, u32[]{:S(2)}) copy-start(s32[1,1,32]{2,1,0:T(1,128)} %param.8) | copy-start | bytes 388
  56.7 1.9 %copy-start = (f32[96,256]{1,0:T(8,128)S(1)}, f32[96,256]{1,0:T(8,128)}, u32[]{:S(2)}) copy-start(f32[96,256]{1,0:T(8,128)} %get-tuple-element.5) | copy-start | bytes 294916

commit v5 on v4

--- a/solution.py
+++ b/solution.py
@@ -330,7 +330,7 @@
             dma((ITERS,)), dma((ITERS,)),
         ],
         compiler_params=pltpu.CompilerParams(
-            collective_id=0, has_side_effects=True, vmem_limit_bytes=60 * 1024 * 1024
+            collective_id=0, has_side_effects=True, vmem_limit_bytes=53 * 1024 * 1024
         ),
     )(table, pixel_factor, date_factor, clear_obs.reshape(cap, BLOCK, BLOCK))
 

time: 59.4 us -> 58 us (0.976)
  Pallas kernels: 54.1 us -> 53.4 us
    pallas_call x1, Pallas kernels: 54.1 us -> 53.4 us  [shards(): pl.pallas_call(body, out_shape=(jax.ShapeDtypeStruct((ru, rank), F32), ja...]
where the time goes in v5:
time: 58 us; the launch traced here: 57.8 us
  Pallas kernels  53.4 us (92%)
  local copies, waits for them, and re-layouts  2.97 us (5%)
  between operations  1.31 us (2%)
    pallas_call x1, Pallas kernels, shards(): pl.pallas_call(body, out_shape=(jax.ShapeDtypeStruct((ru, rank), F32), ja...  53.4 us
    unnamed x6, local copies, waits for them, and re-layouts  2.97 us

profile of v5, /device:TPU:0, one launch (start us, length us, event | category | flops | bytes accessed | tf_op | source)
XLA Modules:
  0.0 57.8 jit_solution(5952469118476669560)
XLA Ops:
  1.3 0.0 copy-start.1
  1.3 0.6 %copy-done.1 = s32[1,1,32]{2,1,0:T(1,128)S(1)} copy-done((s32[1,1,32]{2,1,0:T(1,128)S(1)}, s32[1,1,32]{2,1,0:T(1,128)}, u32[]{:S(2)}) %copy-start.1) | copy-done | bytes 152
  1.9 0.1 select_reduce_fusion.table_ref
  2.0 0.0 copy-start
  2.1 0.9 %copy-done = f32[96,256]{1,0:T(8,128)S(1)} copy-done((f32[96,256]{1,0:T(8,128)S(1)}, f32[96,256]{1,0:T(8,128)}, u32[]{:S(2)}) %copy-start) | copy-done | bytes 98328
  2.9 53.4 %shard_map.68 = (f32[512,256]{1,0:T(8,128)S(1)}, f32[96,256]{1,0:T(8,128)S(1)}) custom-call(s32[96]{0:T(128)S(1)} %select_reduce_fusion.table_ref, f32[512,256]{1,0:T(8,128)} %u_hbm.1, f32[96,256]{1,0:T(8,128)S(1)} %copy-done, bf16[32,128,128]{2,1,0:T(8,128)(2,1)} %bitcast.4), custom_call_target="tpu_custom_call" | custom-call | tf_op jit(solution)/shard_map/pallas_call | solution.py:297
  56.3 0.8 %copy.10 = f32[512,256]{1,0:T(8,128)} copy(f32[512,256]{1,0:T(8,128)S(1)} %get-tuple-element.4) | data formatting | bytes 1048576
  57.1 0.6 %copy.11 = f32[96,256]{1,0:T(8,128)} copy(f32[96,256]{1,0:T(8,128)S(1)} %get-tuple-element.5) | data formatting | bytes 196608
  (1 shorter events, 0.0 us)
Async XLA Ops:
  1.3 0.7 %copy-start.1 = (s32[1,1,32]{2,1,0:T(1,128)S(1)}, s32[1,1,32]{2,1,0:T(1,128)}, u32[]{:S(2)}) copy-start(s32[1,1,32]{2,1,0:T(1,128)} %param.8) | copy-start | bytes 388
  2.0 0.9 %copy-start = (f32[96,256]{1,0:T(8,128)S(1)}, f32[96,256]{1,0:T(8,128)}, u32[]{:S(2)}) copy-start(f32[96,256]{1,0:T(8,128)} %v_hbm.1) | copy-start | bytes 294916
